TPU v7x, 32 devices: a whole 2x2x4 slice. The times are simulated.
32 devices in a mesh: rows: 8 (over y, x, core), cols: 4 (over z).
Axes of the slice: x: 2, y: 2, z: 4, core: 2. Of those that a mesh axis runs over, the one named last changes fastest.
Arguments:
- generator: bfloat16 [2048, 64, 448], P('rows'), may hold values from -0.25 to 0.25
- listed_block_columns: int32 [2048, 7], P('rows'), may hold values from -1 to 2047, as said below
- basis: bfloat16 [131072, 1024], P('rows', 'cols'), may hold values from -0.31445312 to 0.31445312
Outputs:
- projected: float32 [1024, 1024], P('rows', 'cols')
Inputs may be any that keep to these rules, and one draw needn't show every extreme that they name: `listed_block_columns`: entry 0 of each list is its own block-row index i; every other entry is -1 or a block-row index within 128 of i; entries 5 and 6 are i - 128 and i + 128 wherever these lie in 0 to 2047, else -1.
All inputs are finite; a program needn't handle non-finite values.
Results may differ from a plain program's by a relative error of at most 0.0029.
Values may be sent and summed in bfloat16 or wider, within the bound.
A program may use at most 256 MiB of HBM per device.

v0:
```python
import jax
import jax.numpy as jnp
from jax import lax
from jax.sharding import PartitionSpec as P


def extended(value, sides, width):
    for axis, dim in sides:
        count, length = (lax.axis_size(axis), value.shape[dim])
        up = [(i, (i + 1) % count) for i in range(count - 1)]
        down = [(j, i) for i, j in up]
        last = lax.slice_in_dim(value, length - width, length, axis=dim)
        leading = lax.slice_in_dim(value, 0, width, axis=dim)
        before = lax.ppermute(last, axis, up)
        after = lax.ppermute(leading, axis, down)
        value = jnp.concatenate([before, value, after], axis=dim)
    return value


def body(generator, listed_block_columns, basis):
    brows = listed_block_columns.shape[0]
    states = basis.shape[0]
    panel = basis.shape[1]
    bsize = states // brows
    slots = listed_block_columns.shape[1]
    reach = brows // 2
    padded = extended(basis, (("rows", 0),), reach * bsize)
    stacks = padded.reshape(brows + 2 * reach, bsize, panel)
    first = lax.axis_index("rows") * brows - reach
    valid = listed_block_columns >= 0
    safe = jnp.where(valid, listed_block_columns - first, 0)
    selected_columns = stacks[safe]
    selected_columns = jnp.where(
        valid[:, :, None, None], selected_columns, jnp.zeros((), selected_columns.dtype)
    )
    selected_columns = selected_columns.reshape(brows, slots * bsize, panel)
    product = jnp.einsum(
        "bik,bkn->bin", generator, selected_columns, preferred_element_type=jnp.float32
    )
    operator_output = product.reshape(states, panel).astype(jnp.bfloat16)
    row_count = lax.axis_size("rows")
    col_count = lax.axis_size("cols")
    slab_basis, slab_applied = (
        lax.all_to_all(basis, "cols", split_axis=0, concat_axis=1, tiled=True),
        lax.all_to_all(operator_output, "cols", split_axis=0, concat_axis=1, tiled=True),
    )
    basis_width = slab_basis.shape[1]
    left = slab_basis.reshape(slab_basis.shape[0], row_count, basis_width // row_count)
    right = slab_applied.reshape(slab_applied.shape[0], col_count, basis_width // col_count)
    partial_sum = jnp.einsum("sra,scb->rcab", left, right, preferred_element_type=jnp.float32)
    partial_sum = partial_sum.reshape(
        row_count * col_count, basis_width // row_count, basis_width // col_count
    )
    share = lax.psum_scatter(partial_sum, ("rows", "cols"), scatter_dimension=0, tiled=True)
    result = share.reshape(basis_width // row_count, basis_width // col_count)
    return result


def solution(mesh):
    return jax.shard_map(
        body,
        mesh=mesh,
        in_specs=(P("rows", None, None), P("rows", None), P("rows", "cols")),
        out_specs=P("rows", "cols"),
        check_vma=False,
    )
```

profile of v0, /device:TPU:0, one launch (start us, length us, event | category | flops | bytes accessed | tf_op | source)
XLA Modules:
  0.0 616.2 jit_solution(898188104639512890)
XLA Ops:
  6.5 0.0 copy-start
  6.5 5.7 fusion.5
  12.3 4.3 collective-permute-start
  16.6 1.3 collective-permute-start.1
  17.9 5.7 all-to-all-start.1
  23.6 0.0 copy-done
  23.6 0.1 copy.14
  23.8 0.2 reshape.34
  24.0 0.2 copy.13
  24.3 23.4 %copy.15 = bf16[256,64,448]{2,1,0:T(8,128)(2,1)} copy(bf16[256,64,448]{0,2,1:T(8,128)(2,1)} %param.3) | data formatting | bytes 29360128 | tf_op args[0]
  47.7 0.0 collective-permute-done
  47.7 0.0 collective-permute-done.1
  47.7 19.7 %pad_maximum_fusion = bf16[32768,256]{1,0:T(8,128)(2,1)} fusion(bf16[8192,256]{1,0:T(8,128)(2,1)} %collective-permute-done.1, bf16[16384,256]{1,0:T(8,128)(2,1)} %param.5, bf16[8192,256]{1,0:T(8,128)(2,1)} %collective-permute-done), kind=kLoop, calls=%fused_computation.2 | loop fusion | flops 50331648 | bytes 33554432 | tf_op jit(solution)/shard_map/concatenate | solution.py:16
  67.5 45.9 %gather_fusion = bf16[1792,64,256]{2,1,0:T(8,128)(2,1)} fusion(bf16[512,64,256]{2,1,0:T(8,128)(2,1)} %bitcast.29, s32[2048]{0:T(1024)S(1)} %pad_clamp_fusion), kind=kCustom, calls=%fused_computation | custom fusion | bytes 117447680 | tf_op jit(solution)/shard_map/gather | solution.py:32
  113.3 39.6 %bitcast_select_fusion = bf16[256,448,256]{2,1,0:T(8,128)(2,1)} fusion(pred[256,448]{1,0:T(8,128)(4,1)S(1)} %copy.13, bf16[256,448,256]{2,1,0:T(8,128)(2,1)} %bitcast.30), kind=kLoop, calls=%fused_computation.1 | loop fusion | flops 29360128 | bytes 117555200 | tf_op jit(solution)/shard_map/jit(_where)/select_n | solution.py:33
  152.9 28.6 %convolution_convert_fusion = bf16[256,256,64]{1,2,0:T(8,128)(2,1)} fusion(bf16[256,64,448]{2,1,0:T(8,128)(2,1)} %copy.15, bf16[256,448,256]{2,1,0:T(8,128)(2,1)} %bitcast_select_fusion), kind=kOutput, calls=%fused_computation.5 | convolution fusion | flops 3762290688 | bytes 81788928 | tf_op jit(solution)/shard_map/bik,bkn->bin/dot_general | solution.py:37
  181.6 11.4 %copy.16 = bf16[4,4096,256]{1,2,0:T(8,128)(2,1)} copy(bf16[4,4096,256]{2,1,0:T(8,128)(2,1)} %bitcast.32) | data formatting | bytes 16777216 | tf_op jit(solution)/shard_map/convert_element_type | solution.py:40
  192.9 15.3 %all-to-all-done.1 = bf16[4,4096,256]{2,1,0:T(8,128)(2,1)} async-done(((bf16[4,4096,256]{2,1,0:T(8,128)(2,1)}), bf16[4,4096,256]{2,1,0:T(8,128)(2,1)}, u32[]{:S(2)}, u32[]{:S(2)}) %all-to-all-start.1) | async-done | bytes 8388640 | tf_op jit(solution)/shard_map/all_to_all | solution.py:44
  208.2 5.6 all-to-all-start
  213.8 0.2 reduce-scatter.2.cloned.1.call-start
  214.1 11.4 %copy.17 = bf16[4096,4,256]{0,2,1:T(8,128)(2,1)} copy(bf16[4096,4,256]{2,0,1:T(8,128)(2,1)} %bitcast.9) | data formatting | bytes 16777216 | tf_op jit(solution)/shard_map/all_to_all | solution.py:44
  225.5 149.3 %all-to-all-done = bf16[4,4096,256]{1,2,0:T(8,128)(2,1)} async-done(((bf16[4,4096,256]{1,2,0:T(8,128)(2,1)}), bf16[4,4096,256]{1,2,0:T(8,128)(2,1)}, u32[]{:S(2)}, u32[]{:S(2)}) %all-to-all-start) | async-done | bytes 8388640 | tf_op jit(solution)/shard_map/all_to_all | solution.py:45
  374.8 15.0 %fusion.2 = f32[8,4,128,256]{2,3,0,1:T(8,128)} fusion(bf16[4096,8,128,1]{0,2,1,3:T(8,128)(2,1)} %bitcast.34, bf16[4,4096,256]{1,2,0:T(8,128)(2,1)} %all-to-all-done), kind=kOutput, calls=%fused_computation.6 | convolution fusion | flops 8589934592 | bytes 20971520 | tf_op jit(solution)/shard_map/sra,scb->rcab/dot_general | solution.py:50
  389.7 5.4 copy.19
  395.1 0.0 reduce-scatter.2.cloned.1.call-update
  395.1 214.3 %reduce-scatter.2.cloned.1.call-done = f32[1,128,256]{2,1,0:T(8,128)} async-done(((f32[32,128,256]{2,1,0:T(8,128)}), f32[1,128,256]{2,1,0:T(8,128)}) %reduce-scatter.2.cloned.1.call-update) | async-done | bytes 131088 | tf_op jit(solution)/shard_map/reduce_scatter | solution.py:54
  (4 shorter events, 0.1 us)
Async XLA Ops:
  6.5 17.1 %copy-start = (s32[256,7]{0,1:T(8,128)S(1)}, s32[256,7]{0,1:T(8,128)}, u32[]{:S(2)}) copy-start(s32[256,7]{0,1:T(8,128)} %param.4) | copy-start | bytes 21508
  12.3 35.4 %collective-permute-start = (bf16[8192,256]{1,0:T(8,128)(2,1)}, bf16[8192,256]{1,0:T(8,128)(2,1)}, u32[]{:S(2)}, u32[]{:S(2)}) collective-permute-start(bf16[8192,256]{1,0:T(8,128)(2,1)} %get-tuple-element.5), channel_id=1, source_target_pairs={{0,4},{4,8},{8,12},{12,16},{16,20},{20,24},{24,28},{1,5},{5,9},{9,... | collective-permute-start | bytes 12582920 | tf_op jit(solution)/shard_map/ppermute | solution.py:14
  16.6 31.1 %collective-permute-start.1 = (bf16[8192,256]{1,0:T(8,128)(2,1)}, bf16[8192,256]{1,0:T(8,128)(2,1)}, u32[]{:S(2)}, u32[]{:S(2)}) collective-permute-start(bf16[8192,256]{1,0:T(8,128)(2,1)} %get-tuple-element.6), channel_id=1, source_target_pairs={{4,0},{8,4},{12,8},{16,12},{20,16},{24,20},{28,24},{5,1},{9,5},{13... | collective-permute-start | bytes 12582920 | tf_op jit(solution)/shard_map/ppermute | solution.py:15
  17.9 190.3 %all-to-all-start.1 = ((bf16[4,4096,256]{2,1,0:T(8,128)(2,1)}), bf16[4,4096,256]{2,1,0:T(8,128)(2,1)}, u32[]{:S(2)}, u32[]{:S(2)}) async-start(bf16[4,4096,256]{2,1,0:T(8,128)(2,1)} %bitcast.31), calls=%async_computation.1 | async-start | bytes 16777216 | tf_op jit(solution)/shard_map/all_to_all | solution.py:44
  208.2 166.6 %all-to-all-start = ((bf16[4,4096,256]{1,2,0:T(8,128)(2,1)}), bf16[4,4096,256]{1,2,0:T(8,128)(2,1)}, u32[]{:S(2)}, u32[]{:S(2)}) async-start(bf16[4,4096,256]{1,2,0:T(8,128)(2,1)} %copy.16), calls=%async_computation | async-start | bytes 16777216 | tf_op jit(solution)/shard_map/all_to_all | solution.py:45
  213.8 395.5 %reduce-scatter.2.cloned.1.call-start = ((), (), s32[]{:S(2)}) async-start(), calls=%async_computation.3 | async-start | bytes 4325376 | tf_op jit(solution)/shard_map/reduce_scatter | solution.py:54
Sparse Core Ops, SparseCore 0:
  395.2 214.0 reduce-scatter.1
where the time goes:
time: 618 us; the launch traced here: 616 us
  waiting for transfers between devices  379 us (61%)
  local copies, waits for them, and re-layouts  104 us (17%)
  other arithmetic  59.3 us (10%)
  matrix products  43.6 us (7%)
  starting transfers between devices  17.2 us (3%)
  between operations  13.5 us (2%)
    reduce_scatter x1, waiting for transfers between devices, body(): lax.psum_scatter(partial_sum, ('rows', 'cols'), scatter_dimension=0, tile...  214 us
    all_to_all x1, waiting for transfers between devices, body(): lax.all_to_all(operator_output, 'cols', split_axis=0, concat_axis=1, tile...  149 us
    gather x1, local copies, waits for them, and re-layouts, body(): selected_columns = stacks[safe]  45.9 us
    select_n x1, other arithmetic, body(): jnp.where(valid[:, :, None, None], selected_columns, jnp.zeros((), select...  39.6 us
    dot_general x1, matrix products, body(): jnp.einsum('bik,bkn->bin', generator, selected_columns, preferred_element...  28.6 us
    unnamed x3, local copies, waits for them, and re-layouts  23.4 us
    concatenate x1, other arithmetic, extended(): value = jnp.concatenate([before, value, after], axis=dim)  19.7 us
    all_to_all x1, waiting for transfers between devices, body(): lax.all_to_all(basis, 'cols', split_axis=0, concat_axis=1, tiled=True)  15.3 us
  transfers between devices with their start and end apart: 5, of which 3 were waited for; matrix products, arithmetic and copies ran while one was open for 29% of the time, Pallas kernels for 0%

commit v1 on v0

v1 whole, which is shorter than its diff:
```python
import functools

import jax
import jax.numpy as jnp
from jax import lax
from jax.experimental import pallas as pl
from jax.experimental.pallas import tpu as pltpu
from jax.sharding import PartitionSpec as P

VMEM_LIMIT = 56 * 1024 * 1024


def apply_kernel(index, before, own, after, generator, applied, stacks, sems, *, bsize, slots, group):
    step = pl.program_id(0)
    low, mid = before.shape[0], own.shape[0]
    high = after.shape[0]

    @pl.when(step == 0)
    def _():
        copies = [
            pltpu.make_async_copy(before, stacks.at[pl.ds(0, low)], sems.at[0]),
            pltpu.make_async_copy(own, stacks.at[pl.ds(low, mid)], sems.at[1]),
            pltpu.make_async_copy(after, stacks.at[pl.ds(low + mid, high)], sems.at[2]),
        ]
        for copy in copies:
            copy.start()
        stacks[pl.ds(low + mid + high, bsize), :] = jnp.zeros((bsize, own.shape[1]), own.dtype)
        for copy in copies:
            copy.wait()

    for g in range(group):
        base = (step * group + g) * slots
        blocks = [
            stacks[pl.ds(pl.multiple_of(index[base + s] * bsize, bsize), bsize), :] for s in range(slots)
        ]
        total = jnp.dot(generator[g], jnp.concatenate(blocks, axis=0), preferred_element_type=jnp.float32)
        applied[g * bsize : (g + 1) * bsize, :] = total.astype(applied.dtype)


def apply_blocks(index, before, own, after, generator):
    brows, bsize, width = generator.shape
    slots = width // bsize
    panel = own.shape[1]
    group = 16
    rows = before.shape[0] + own.shape[0] + after.shape[0] + bsize
    anywhere = pl.BlockSpec(memory_space=pl.ANY)
    return pl.pallas_call(
        functools.partial(apply_kernel, bsize=bsize, slots=slots, group=group),
        grid_spec=pltpu.PrefetchScalarGridSpec(
            num_scalar_prefetch=1,
            grid=(brows // group,),
            in_specs=[anywhere, anywhere, anywhere, pl.BlockSpec((group, bsize, width), lambda i, index: (i, 0, 0))],
            out_specs=pl.BlockSpec((group * bsize, panel), lambda i, index: (i, 0)),
            scratch_shapes=[pltpu.VMEM((rows, panel), own.dtype), pltpu.SemaphoreType.DMA((3,))],
        ),
        out_shape=jax.ShapeDtypeStruct(own.shape, own.dtype),
        compiler_params=pltpu.CompilerParams(vmem_limit_bytes=VMEM_LIMIT),
        cost_estimate=pl.CostEstimate(
            flops=2 * brows * bsize * width * panel, bytes_accessed=48 * 1024 * 1024, transcendentals=0
        ),
    )(index, before, own, after, generator)


def product_kernel(left, right, out, total):
    step = pl.program_id(0)
    panels = left.shape[0]

    @pl.when(step == 0)
    def _():
        total[...] = jnp.zeros_like(total)

    rights = jnp.concatenate([right[c] for c in range(right.shape[0])], axis=1)
    panel = left.shape[2]
    for c in range(panels):
        total[c * panel : (c + 1) * panel, :] += lax.dot_general(
            left[c], rights, (((0,), (0,)), ((), ())), preferred_element_type=jnp.float32
        )

    @pl.when(step == pl.num_programs(0) - 1)
    def _():
        height, width = out.shape[2], out.shape[3]
        for r in range(out.shape[0]):
            for c in range(out.shape[1]):
                out[r, c] = total[r * height : (r + 1) * height, c * width : (c + 1) * width].astype(out.dtype)


def product(left, right, row_count, col_count):
    panels, depth, panel = left.shape
    width = panels * panel
    tile = 512
    spec = pl.BlockSpec((panels, tile, panel), lambda i: (0, i, 0))
    shape = (row_count, col_count, width // row_count, width // col_count)
    return pl.pallas_call(
        product_kernel,
        grid=(depth // tile,),
        in_specs=[spec, spec],
        out_specs=pl.BlockSpec(shape, lambda i: (0, 0, 0, 0)),
        out_shape=jax.ShapeDtypeStruct(shape, jnp.bfloat16),
        scratch_shapes=[pltpu.VMEM((width, width), jnp.float32)],
        compiler_params=pltpu.CompilerParams(vmem_limit_bytes=VMEM_LIMIT),
        cost_estimate=pl.CostEstimate(
            flops=2 * depth * width * width, bytes_accessed=20 * 1024 * 1024, transcendentals=0
        ),
    )(left, right)


def body(generator, listed_block_columns, basis):
    brows, bsize, _ = generator.shape
    states, panel = basis.shape
    reach = brows // 2
    width = reach * bsize
    row_count = lax.axis_size("rows")
    col_count = lax.axis_size("cols")
    up = [(i, i + 1) for i in range(row_count - 1)]
    down = [(j, i) for i, j in up]
    before = lax.ppermute(basis[states - width :], "rows", up)
    after = lax.ppermute(basis[:width], "rows", down)

    first = lax.axis_index("rows") * brows - reach
    index = jnp.where(listed_block_columns >= 0, listed_block_columns - first, brows + 2 * reach).reshape(-1)

    def spread(value):
        parts = value.reshape(col_count, states // col_count, panel)
        return lax.all_to_all(parts, "cols", split_axis=0, concat_axis=0)

    slab_basis = spread(basis)
    applied = apply_blocks(index, before, basis, after, generator)
    slab_applied = spread(applied)
    partial = product(slab_basis, slab_applied, row_count, col_count)
    shares = lax.all_to_all(partial, "rows", split_axis=0, concat_axis=0)
    share = jnp.sum(shares.astype(jnp.float32), axis=0)
    pieces = lax.all_to_all(share, "cols", split_axis=0, concat_axis=0)
    return jnp.sum(pieces, axis=0)


def solution(mesh):
    return jax.shard_map(
        body,
        mesh=mesh,
        in_specs=(P("rows", None, None), P("rows", None), P("rows", "cols")),
        out_specs=P("rows", "cols"),
        check_vma=False,
    )
```

time: 618 us -> 445 us (0.72)
  waiting for transfers between devices: 379 us -> 123 us
  blocking collectives: 0 us -> 237 us
  local copies, waits for them, and re-layouts: 104 us -> 29.8 us
  other arithmetic: 59.3 us -> 0.97 us
  matrix products: 43.6 us -> 0 us
  Pallas kernels: 0 us -> 40.7 us
  between operations: 13.5 us -> 0.05 us
    all_to_all x0 -> x3, blocking collectives: none -> 237 us  [the longest x1 190 us: spread(): return lax.all_to_all(parts, 'cols', split_axis=0, concat_axis=0)]
    reduce_scatter x1 -> x0, waiting for transfers between devices: 214 us -> none  [body(): lax.psum_scatter(partial_sum, ('rows', 'cols'), scatter_dimension=0, tile...]
    gather x1 -> x0, local copies, waits for them, and re-layouts: 45.9 us -> none  [body(): selected_columns = stacks[safe]]
    dot_general x2 -> x0, matrix products: 43.6 us -> none  [the longest x1 28.6 us: body(): jnp.einsum('bik,bkn->bin', generator, selected_columns, preferred_element...]
    all_to_all x2 -> x1, waiting for transfers between devices: 165 us -> 123 us  [spread(): return lax.all_to_all(parts, 'cols', split_axis=0, concat_axis=0)]
    pallas_call x0 -> x2, Pallas kernels: none -> 40.7 us  [the longest x1 26.1 us: apply_blocks(): pl.pallas_call(functools.partial(apply_kernel, bsize=bsize, slots=slots,...]
    select_n x2 -> x1, other arithmetic: 39.6 us -> 0.01 us  [body(): jnp.where(listed_block_columns >= 0, listed_block_columns - first, brows...]
    concatenate x1 -> x0, other arithmetic: 19.7 us -> none  [extended(): value = jnp.concatenate([before, value, after], axis=dim)]
  transfers between devices with their start and end apart: 5 -> 3, of which waited for: 3 -> 1; matrix products, arithmetic and copies ran while one was open for 29% -> 7% of each run, Pallas kernels for 0% -> 6%
where the time goes in v1:
time: 445 us; the launch traced here: 443 us
  blocking collectives  237 us (53%)
  waiting for transfers between devices  123 us (28%)
  Pallas kernels  40.7 us (9%)
  local copies, waits for them, and re-layouts  29.8 us (7%)
  starting transfers between devices  11.3 us (3%)
    all_to_all x1, blocking collectives, spread(): return lax.all_to_all(parts, 'cols', split_axis=0, concat_axis=0)  190 us
    all_to_all x1, waiting for transfers between devices, spread(): return lax.all_to_all(parts, 'cols', split_axis=0, concat_axis=0)  123 us
    all_to_all x1, blocking collectives, body(): shares = lax.all_to_all(partial, 'rows', split_axis=0, concat_axis=0)  30.5 us
    pallas_call x1, Pallas kernels, apply_blocks(): pl.pallas_call(functools.partial(apply_kernel, bsize=bsize, slots=slots,...  26.1 us
    unnamed x3, local copies, waits for them, and re-layouts  23.2 us
    all_to_all x1, blocking collectives, body(): pieces = lax.all_to_all(share, 'cols', split_axis=0, concat_axis=0)  16.5 us
    pallas_call x1, Pallas kernels, product(): pl.pallas_call(product_kernel, grid=(depth // tile,), in_specs=[spec, spe...  14.6 us
  transfers between devices with their start and end apart: 3, of which 1 were waited for; matrix products, arithmetic and copies ran while one was open for 7% of the time, Pallas kernels for 6%

profile of v1, /device:TPU:0, one launch (start us, length us, event | category | flops | bytes accessed | tf_op | source)
XLA Modules:
  0.0 443.2 jit_solution(4380943124984111365)
XLA Ops:
  0.0 6.3 %all-to-all-start = ((bf16[4,4096,256]{2,1,0:T(8,128)(2,1)}), bf16[4,4096,256]{2,1,0:T(8,128)(2,1)}, u32[]{:S(2)}, u32[]{:S(2)}) async-start(bf16[4,4096,256]{2,1,0:T(8,128)(2,1)} %bitcast.2), calls=%async_computation | async-start | bytes 16777216 | tf_op jit(solution)/shard_map/all_to_all | solution.py:124
  6.3 5.7 %fusion = (bf16[8192,256]{1,0:T(8,128)(2,1)}, bf16[8192,256]{1,0:T(8,128)(2,1)}) fusion(bf16[16384,256]{1,0:T(8,128)(2,1)} %own.1), kind=kLoop, calls=%fused_computation.2 | loop fusion | bytes 16777216 | tf_op jit(solution)/shard_map/slice | solution.py:117
  12.0 3.7 collective-permute-start
  15.7 1.3 collective-permute-start.1
  17.0 0.0 copy-start
  17.1 23.2 %copy.8.generator = bf16[256,64,448]{2,1,0:T(8,128)(2,1)} copy(bf16[256,64,448]{0,2,1:T(8,128)(2,1)} %param.3) | data formatting | bytes 29360128 | tf_op args[0]
  40.3 0.0 copy-done
  40.3 0.1 copy.7
  40.4 0.8 reshape.10.index
  41.2 0.0 collective-permute-done.before
  41.2 0.0 collective-permute-done.1.after
  41.2 26.1 %shard_map.37 = bf16[16384,256]{1,0:T(8,128)(2,1)} custom-call(s32[1792]{0:T(1024)} %reshape.10.index, bf16[8192,256]{1,0:T(8,128)(2,1)} %collective-permute-done.before, bf16[16384,256]{1,0:T(8,128)(2,1)} %own.1, bf16[8192,256]{1,0:T(8,128)(2,1)} %collective-permute-done.1.after, bf16[256,64,448]{2,1,0:T(8,128)(2,1)} %copy.8.generator), custom_call_target="tpu_custom_call" | custom-call | flops 3758096384 | bytes 50331648 | tf_op jit(solution)/shard_map/pallas_call | solution.py:47
  67.3 123.1 %all-to-all-done.left = bf16[4,4096,256]{2,1,0:T(8,128)(2,1)} async-done(((bf16[4,4096,256]{2,1,0:T(8,128)(2,1)}), bf16[4,4096,256]{2,1,0:T(8,128)(2,1)}, u32[]{:S(2)}, u32[]{:S(2)}) %all-to-all-start) | async-done | bytes 8388640 | tf_op jit(solution)/shard_map/all_to_all | solution.py:124
  190.4 190.2 %all_to_all.20.right = bf16[4,4096,256]{2,1,0:T(8,128)(2,1)} all-to-all(bf16[4,4096,256]{2,1,0:T(8,128)(2,1)} %bitcast.3), channel_id=1, replica_groups=mesh['rows'=8,'cols'=4] {'cols'}, dimensions={0} | all-to-all | bytes 16777216 | tf_op jit(solution)/shard_map/all_to_all | solution.py:124
  380.6 14.6 %shard_map.38 = bf16[8,4,128,256]{3,2,1,0:T(8,128)(2,1)} custom-call(bf16[4,4096,256]{2,1,0:T(8,128)(2,1)} %all-to-all-done.left, bf16[4,4096,256]{2,1,0:T(8,128)(2,1)} %all_to_all.20.right), custom_call_target="tpu_custom_call" | custom-call | flops 8589934592 | bytes 20971520 | tf_op jit(solution)/shard_map/pallas_call | solution.py:93
  395.2 30.5 %all_to_all.21 = bf16[8,4,128,256]{3,2,1,0:T(8,128)(2,1)S(1)} all-to-all(bf16[8,4,128,256]{3,2,1,0:T(8,128)(2,1)} %shard_map.38), channel_id=1, replica_groups=mesh['rows'=8,'cols'=4] {'rows'}, dimensions={0} | all-to-all | bytes 4194304 | tf_op jit(solution)/shard_map/all_to_all | solution.py:130
  425.8 0.3 convert_reduce_fusion
  426.0 16.5 %all_to_all.22 = f32[4,128,256]{2,1,0:T(8,128)S(1)} all-to-all(f32[4,128,256]{2,1,0:T(8,128)S(1)} %convert_reduce_fusion), channel_id=1, replica_groups=mesh['rows'=8,'cols'=4] {'cols'}, dimensions={0} | all-to-all | bytes 1048576 | tf_op jit(solution)/shard_map/all_to_all | solution.py:132
  442.6 0.7 reduce_sum.19
  (1 shorter events, 0.0 us)
Async XLA Ops:
  0.0 190.4 %all-to-all-start = ((bf16[4,4096,256]{2,1,0:T(8,128)(2,1)}), bf16[4,4096,256]{2,1,0:T(8,128)(2,1)}, u32[]{:S(2)}, u32[]{:S(2)}) async-start(bf16[4,4096,256]{2,1,0:T(8,128)(2,1)} %bitcast.2), calls=%async_computation | async-start | bytes 16777216 | tf_op jit(solution)/shard_map/all_to_all | solution.py:124
  12.0 29.2 %collective-permute-start = (bf16[8192,256]{1,0:T(8,128)(2,1)}, bf16[8192,256]{1,0:T(8,128)(2,1)}, u32[]{:S(2)}, u32[]{:S(2)}) collective-permute-start(bf16[8192,256]{1,0:T(8,128)(2,1)} %get-tuple-element.6), channel_id=1, source_target_pairs={{0,4},{4,8},{8,12},{12,16},{16,20},{20,24},{24,28},{1,5},{5,9},{9,... | collective-permute-start | bytes 12582920 | tf_op jit(solution)/shard_map/ppermute | solution.py:116
  15.7 25.5 %collective-permute-start.1 = (bf16[8192,256]{1,0:T(8,128)(2,1)}, bf16[8192,256]{1,0:T(8,128)(2,1)}, u32[]{:S(2)}, u32[]{:S(2)}) collective-permute-start(bf16[8192,256]{1,0:T(8,128)(2,1)} %get-tuple-element.5), channel_id=1, source_target_pairs={{4,0},{8,4},{12,8},{16,12},{20,16},{24,20},{28,24},{5,1},{9,5},{13... | collective-permute-start | bytes 12582920 | tf_op jit(solution)/shard_map/ppermute | solution.py:117
  17.0 23.2 %copy-start = (s32[256,7]{0,1:T(8,128)S(1)}, s32[256,7]{0,1:T(8,128)}, u32[]{:S(2)}) copy-start(s32[256,7]{0,1:T(8,128)} %param.4) | copy-start | bytes 21508

commit v2 on v1

--- a/solution.py
+++ b/solution.py
@@ -87,7 +87,7 @@
 def product(left, right, row_count, col_count):
     panels, depth, panel = left.shape
     width = panels * panel
-    tile = 512
+    tile = 1024
     spec = pl.BlockSpec((panels, tile, panel), lambda i: (0, i, 0))
     shape = (row_count, col_count, width // row_count, width // col_count)
     return pl.pallas_call(

time: 445 us -> 444 us (level)
  no operation moved by 1% of the time
where the time goes in v2:
time: 444 us; the launch traced here: 442 us
  blocking collectives  237 us (53%)
  waiting for transfers between devices  123 us (28%)
  Pallas kernels  39.7 us (9%)
  local copies, waits for them, and re-layouts  29.8 us (7%)
  starting transfers between devices  11.3 us (3%)
    all_to_all x1, blocking collectives, spread(): return lax.all_to_all(parts, 'cols', split_axis=0, concat_axis=0)  190 us
    all_to_all x1, waiting for transfers between devices, spread(): return lax.all_to_all(parts, 'cols', split_axis=0, concat_axis=0)  123 us
    all_to_all x1, blocking collectives, body(): shares = lax.all_to_all(partial, 'rows', split_axis=0, concat_axis=0)  30.5 us
    pallas_call x1, Pallas kernels, apply_blocks(): pl.pallas_call(functools.partial(apply_kernel, bsize=bsize, slots=slots,...  26.1 us
    unnamed x3, local copies, waits for them, and re-layouts  23.2 us
    all_to_all x1, blocking collectives, body(): pieces = lax.all_to_all(share, 'cols', split_axis=0, concat_axis=0)  16.5 us
    pallas_call x1, Pallas kernels, product(): pl.pallas_call(product_kernel, grid=(depth // tile,), in_specs=[spec, spe...  13.6 us
  transfers between devices with their start and end apart: 3, of which 1 were waited for; matrix products, arithmetic and copies ran while one was open for 7% of the time, Pallas kernels for 6%

profile of v2, /device:TPU:0, one launch (start us, length us, event | category | flops | bytes accessed | tf_op | source)
XLA Modules:
  0.0 442.3 jit_solution(781324080036659151)
XLA Ops:
  0.0 6.3 %all-to-all-start = ((bf16[4,4096,256]{2,1,0:T(8,128)(2,1)}), bf16[4,4096,256]{2,1,0:T(8,128)(2,1)}, u32[]{:S(2)}, u32[]{:S(2)}) async-start(bf16[4,4096,256]{2,1,0:T(8,128)(2,1)} %bitcast.2), calls=%async_computation | async-start | bytes 16777216 | tf_op jit(solution)/shard_map/all_to_all | solution.py:124
  6.3 5.7 %fusion = (bf16[8192,256]{1,0:T(8,128)(2,1)}, bf16[8192,256]{1,0:T(8,128)(2,1)}) fusion(bf16[16384,256]{1,0:T(8,128)(2,1)} %own.1), kind=kLoop, calls=%fused_computation.2 | loop fusion | bytes 16777216 | tf_op jit(solution)/shard_map/slice | solution.py:117
  12.0 3.7 collective-permute-start
  15.7 1.3 collective-permute-start.1
  17.0 0.0 copy-start
  17.1 23.2 %copy.8.generator = bf16[256,64,448]{2,1,0:T(8,128)(2,1)} copy(bf16[256,64,448]{0,2,1:T(8,128)(2,1)} %param.3) | data formatting | bytes 29360128 | tf_op args[0]
  40.3 0.0 copy-done
  40.3 0.1 copy.7
  40.4 0.8 reshape.10.index
  41.2 0.0 collective-permute-done.before
  41.2 0.0 collective-permute-done.1.after
  41.2 26.1 %shard_map.37 = bf16[16384,256]{1,0:T(8,128)(2,1)} custom-call(s32[1792]{0:T(1024)} %reshape.10.index, bf16[8192,256]{1,0:T(8,128)(2,1)} %collective-permute-done.before, bf16[16384,256]{1,0:T(8,128)(2,1)} %own.1, bf16[8192,256]{1,0:T(8,128)(2,1)} %collective-permute-done.1.after, bf16[256,64,448]{2,1,0:T(8,128)(2,1)} %copy.8.generator), custom_call_target="tpu_custom_call" | custom-call | flops 3758096384 | bytes 50331648 | tf_op jit(solution)/shard_map/pallas_call | solution.py:47
  67.3 123.1 %all-to-all-done.left = bf16[4,4096,256]{2,1,0:T(8,128)(2,1)} async-done(((bf16[4,4096,256]{2,1,0:T(8,128)(2,1)}), bf16[4,4096,256]{2,1,0:T(8,128)(2,1)}, u32[]{:S(2)}, u32[]{:S(2)}) %all-to-all-start) | async-done | bytes 8388640 | tf_op jit(solution)/shard_map/all_to_all | solution.py:124
  190.4 190.2 %all_to_all.20.right = bf16[4,4096,256]{2,1,0:T(8,128)(2,1)} all-to-all(bf16[4,4096,256]{2,1,0:T(8,128)(2,1)} %bitcast.3), channel_id=1, replica_groups=mesh['rows'=8,'cols'=4] {'cols'}, dimensions={0} | all-to-all | bytes 16777216 | tf_op jit(solution)/shard_map/all_to_all | solution.py:124
  380.6 13.6 %shard_map.38 = bf16[8,4,128,256]{3,2,1,0:T(8,128)(2,1)} custom-call(bf16[4,4096,256]{2,1,0:T(8,128)(2,1)} %all-to-all-done.left, bf16[4,4096,256]{2,1,0:T(8,128)(2,1)} %all_to_all.20.right), custom_call_target="tpu_custom_call" | custom-call | flops 8589934592 | bytes 20971520 | tf_op jit(solution)/shard_map/pallas_call | solution.py:93
  394.2 30.5 %all_to_all.21 = bf16[8,4,128,256]{3,2,1,0:T(8,128)(2,1)S(1)} all-to-all(bf16[8,4,128,256]{3,2,1,0:T(8,128)(2,1)} %shard_map.38), channel_id=1, replica_groups=mesh['rows'=8,'cols'=4] {'rows'}, dimensions={0} | all-to-all | bytes 4194304 | tf_op jit(solution)/shard_map/all_to_all | solution.py:130
  424.8 0.3 convert_reduce_fusion
  425.1 16.5 %all_to_all.22 = f32[4,128,256]{2,1,0:T(8,128)S(1)} all-to-all(f32[4,128,256]{2,1,0:T(8,128)S(1)} %convert_reduce_fusion), channel_id=1, replica_groups=mesh['rows'=8,'cols'=4] {'cols'}, dimensions={0} | all-to-all | bytes 1048576 | tf_op jit(solution)/shard_map/all_to_all | solution.py:132
  441.6 0.7 reduce_sum.19
  (1 shorter events, 0.0 us)
Async XLA Ops:
  0.0 190.4 %all-to-all-start = ((bf16[4,4096,256]{2,1,0:T(8,128)(2,1)}), bf16[4,4096,256]{2,1,0:T(8,128)(2,1)}, u32[]{:S(2)}, u32[]{:S(2)}) async-start(bf16[4,4096,256]{2,1,0:T(8,128)(2,1)} %bitcast.2), calls=%async_computation | async-start | bytes 16777216 | tf_op jit(solution)/shard_map/all_to_all | solution.py:124
  12.0 29.2 %collective-permute-start = (bf16[8192,256]{1,0:T(8,128)(2,1)}, bf16[8192,256]{1,0:T(8,128)(2,1)}, u32[]{:S(2)}, u32[]{:S(2)}) collective-permute-start(bf16[8192,256]{1,0:T(8,128)(2,1)} %get-tuple-element.6), channel_id=1, source_target_pairs={{0,4},{4,8},{8,12},{12,16},{16,20},{20,24},{24,28},{1,5},{5,9},{9,... | collective-permute-start | bytes 12582920 | tf_op jit(solution)/shard_map/ppermute | solution.py:116
  15.7 25.5 %collective-permute-start.1 = (bf16[8192,256]{1,0:T(8,128)(2,1)}, bf16[8192,256]{1,0:T(8,128)(2,1)}, u32[]{:S(2)}, u32[]{:S(2)}) collective-permute-start(bf16[8192,256]{1,0:T(8,128)(2,1)} %get-tuple-element.5), channel_id=1, source_target_pairs={{4,0},{8,4},{12,8},{16,12},{20,16},{24,20},{28,24},{5,1},{9,5},{13... | collective-permute-start | bytes 12582920 | tf_op jit(solution)/shard_map/ppermute | solution.py:117
  17.0 23.2 %copy-start = (s32[256,7]{0,1:T(8,128)S(1)}, s32[256,7]{0,1:T(8,128)}, u32[]{:S(2)}) copy-start(s32[256,7]{0,1:T(8,128)} %param.4) | copy-start | bytes 21508

commit v3 on v2

--- a/solution.py
+++ b/solution.py
@@ -10,7 +10,8 @@
 VMEM_LIMIT = 56 * 1024 * 1024
 
 
-def apply_kernel(index, before, own, after, generator, applied, stacks, sems, *, bsize, slots, group):
+def apply_kernel(index, before, own, after, generator, *rest, bsize, slots, group):
+    *parts, stacks, sems = rest
     step = pl.program_id(0)
     low, mid = before.shape[0], own.shape[0]
     high = after.shape[0]
@@ -34,10 +35,12 @@
             stacks[pl.ds(pl.multiple_of(index[base + s] * bsize, bsize), bsize), :] for s in range(slots)
         ]
         total = jnp.dot(generator[g], jnp.concatenate(blocks, axis=0), preferred_element_type=jnp.float32)
-        applied[g * bsize : (g + 1) * bsize, :] = total.astype(applied.dtype)
+        width = total.shape[1] // len(parts)
+        for p, applied in enumerate(parts):
+            applied[g * bsize : (g + 1) * bsize, :] = total[:, p * width : (p + 1) * width].astype(applied.dtype)
 
 
-def apply_blocks(index, before, own, after, generator):
+def apply_blocks(index, before, own, after, generator, count):
     brows, bsize, width = generator.shape
     slots = width // bsize
     panel = own.shape[1]
@@ -50,10 +53,10 @@
             num_scalar_prefetch=1,
             grid=(brows // group,),
             in_specs=[anywhere, anywhere, anywhere, pl.BlockSpec((group, bsize, width), lambda i, index: (i, 0, 0))],
-            out_specs=pl.BlockSpec((group * bsize, panel), lambda i, index: (i, 0)),
+            out_specs=[pl.BlockSpec((group * bsize, panel // count), lambda i, index: (i, 0))] * count,
             scratch_shapes=[pltpu.VMEM((rows, panel), own.dtype), pltpu.SemaphoreType.DMA((3,))],
         ),
-        out_shape=jax.ShapeDtypeStruct(own.shape, own.dtype),
+        out_shape=[jax.ShapeDtypeStruct((own.shape[0], panel // count), own.dtype)] * count,
         compiler_params=pltpu.CompilerParams(vmem_limit_bytes=VMEM_LIMIT),
         cost_estimate=pl.CostEstimate(
             flops=2 * brows * bsize * width * panel, bytes_accessed=48 * 1024 * 1024, transcendentals=0
@@ -87,19 +90,20 @@
 def product(left, right, row_count, col_count):
     panels, depth, panel = left.shape
     width = panels * panel
+    wide = panels * right.shape[2]
     tile = 1024
-    spec = pl.BlockSpec((panels, tile, panel), lambda i: (0, i, 0))
-    shape = (row_count, col_count, width // row_count, width // col_count)
+    specs = [pl.BlockSpec((panels, tile, v.shape[2]), lambda i: (0, i, 0)) for v in (left, right)]
+    shape = (row_count, col_count, width // row_count, wide // col_count)
     return pl.pallas_call(
         product_kernel,
         grid=(depth // tile,),
-        in_specs=[spec, spec],
+        in_specs=specs,
         out_specs=pl.BlockSpec(shape, lambda i: (0, 0, 0, 0)),
         out_shape=jax.ShapeDtypeStruct(shape, jnp.bfloat16),
-        scratch_shapes=[pltpu.VMEM((width, width), jnp.float32)],
+        scratch_shapes=[pltpu.VMEM((width, wide), jnp.float32)],
         compiler_params=pltpu.CompilerParams(vmem_limit_bytes=VMEM_LIMIT),
         cost_estimate=pl.CostEstimate(
-            flops=2 * depth * width * width, bytes_accessed=20 * 1024 * 1024, transcendentals=0
+            flops=2 * depth * width * wide, bytes_accessed=20 * 1024 * 1024, transcendentals=0
         ),
     )(left, right)
 
@@ -120,15 +124,38 @@
     index = jnp.where(listed_block_columns >= 0, listed_block_columns - first, brows + 2 * reach).reshape(-1)
 
     def spread(value):
-        parts = value.reshape(col_count, states // col_count, panel)
+        parts = value.reshape(col_count, states // col_count, value.shape[1])
         return lax.all_to_all(parts, "cols", split_axis=0, concat_axis=0)
 
     slab_basis = spread(basis)
-    applied = apply_blocks(index, before, basis, after, generator)
-    slab_applied = spread(applied)
-    partial = product(slab_basis, slab_applied, row_count, col_count)
-    shares = lax.all_to_all(partial, "rows", split_axis=0, concat_axis=0)
-    share = jnp.sum(shares.astype(jnp.float32), axis=0)
+    count = max(1, panel // 128)
+    results = []
+    slabs = []
+    held = slab_basis
+    for part in apply_blocks(index, before, basis, after, generator, count):
+        part, held = lax.optimization_barrier((part, held))
+        if not slabs:
+            slab_basis = held
+        else:
+            slabs[-1] = held
+        held = spread(part)
+        slabs.append(held)
+    me = lax.axis_index("rows")
+    for p, slab in enumerate(slabs):
+        if results:
+            slab, results[-1] = lax.optimization_barrier((slab, results[-1]))
+        partial = product(slab_basis, slab, row_count, col_count)
+        if p + 1 < count:
+            mine = lax.dynamic_index_in_dim(partial, me, 0, keepdims=False).astype(jnp.float32)
+            for away in range(1, row_count):
+                piece = lax.dynamic_index_in_dim(partial, lax.rem(me + away, row_count), 0, keepdims=False)
+                pairs = [(i, (i + away) % row_count) for i in range(row_count)]
+                mine += lax.ppermute(piece, "rows", pairs).astype(jnp.float32)
+        else:
+            shares = lax.all_to_all(partial, "rows", split_axis=0, concat_axis=0)
+            mine = jnp.sum(shares.astype(jnp.float32), axis=0)
+        results.append(mine)
+    share = jnp.concatenate(results, axis=2)
     pieces = lax.all_to_all(share, "cols", split_axis=0, concat_axis=0)
     return jnp.sum(pieces, axis=0)
 

time: 444 us -> 433 us (0.975)
  blocking collectives: 237 us -> 134 us
  waiting for transfers between devices: 123 us -> 198 us
  starting transfers between devices: 11.3 us -> 22 us
    all_to_all x1, blocking collectives: 190 us -> 98.5 us  [spread(): return lax.all_to_all(parts, 'cols', split_axis=0, concat_axis=0)]
    all_to_all x1 -> x2, waiting for transfers between devices: 123 us -> 187 us  [spread(): return lax.all_to_all(parts, 'cols', split_axis=0, concat_axis=0)]
    all_to_all x1, blocking collectives: 30.5 us -> 19 us  [body(): shares = lax.all_to_all(partial, 'rows', split_axis=0, concat_axis=0)]
    ppermute x0 -> x7, waiting for transfers between devices: none -> 11 us  [body(): mine += lax.ppermute(piece, 'rows', pairs).astype(jnp.float32)]
    ppermute x0 -> x7, starting transfers between devices: none -> 5.99 us  [body(): mine += lax.ppermute(piece, 'rows', pairs).astype(jnp.float32)]
    all_to_all x1 -> x2, starting transfers between devices: 6.32 us -> 11.2 us  [spread(): return lax.all_to_all(parts, 'cols', split_axis=0, concat_axis=0)]
    pallas_call x1 -> x2, Pallas kernels: 13.6 us -> 17.9 us  [product(): pl.pallas_call(product_kernel, grid=(depth // tile,), in_specs=specs, out...]
  transfers between devices with their start and end apart: 3 -> 11, of which waited for: 1 -> 5; matrix products, arithmetic and copies ran while one was open for 7% -> 8% of each run, Pallas kernels for 6% -> 8%
where the time goes in v3:
time: 433 us; the launch traced here: 431 us
  waiting for transfers between devices  198 us (46%)
  blocking collectives  134 us (31%)
  Pallas kernels  44 us (10%)
  local copies, waits for them, and re-layouts  31.5 us (7%)
  starting transfers between devices  22 us (5%)
    all_to_all x2, waiting for transfers between devices, spread(): return lax.all_to_all(parts, 'cols', split_axis=0, concat_axis=0)  187 us
    all_to_all x1, blocking collectives, spread(): return lax.all_to_all(parts, 'cols', split_axis=0, concat_axis=0)  98.5 us
    pallas_call x1, Pallas kernels, apply_blocks(): pl.pallas_call(functools.partial(apply_kernel, bsize=bsize, slots=slots,...  26.1 us
    unnamed x3, local copies, waits for them, and re-layouts  23.4 us
    all_to_all x1, blocking collectives, body(): shares = lax.all_to_all(partial, 'rows', split_axis=0, concat_axis=0)  19 us
    pallas_call x2, Pallas kernels, product(): pl.pallas_call(product_kernel, grid=(depth // tile,), in_specs=specs, out...  17.9 us
    all_to_all x1, blocking collectives, body(): pieces = lax.all_to_all(share, 'cols', split_axis=0, concat_axis=0)  16.5 us
    all_to_all x2, starting transfers between devices, spread(): return lax.all_to_all(parts, 'cols', split_axis=0, concat_axis=0)  11.2 us
  transfers between devices with their start and end apart: 11, of which 5 were waited for; matrix products, arithmetic and copies ran while one was open for 8% of the time, Pallas kernels for 8%

profile of v3, /device:TPU:0, one launch (start us, length us, event | category | flops | bytes accessed | tf_op | source)
XLA Modules:
  0.0 431.4 jit_solution(963973521241470797)
XLA Ops:
  0.0 6.3 %all-to-all-start = ((bf16[4,4096,256]{2,1,0:T(8,128)(2,1)}), bf16[4,4096,256]{2,1,0:T(8,128)(2,1)}, u32[]{:S(2)}, u32[]{:S(2)}) async-start(bf16[4,4096,256]{2,1,0:T(8,128)(2,1)} %bitcast.20), calls=%async_computation | async-start | bytes 16777216 | tf_op jit(solution)/shard_map/all_to_all | solution.py:128
  6.3 5.8 %fusion.6 = (bf16[8192,256]{1,0:T(8,128)(2,1)}, bf16[8192,256]{1,0:T(8,128)(2,1)}) fusion(bf16[16384,256]{1,0:T(8,128)(2,1)} %own.1), kind=kLoop, calls=%fused_computation.17 | loop fusion | bytes 16777216 | tf_op jit(solution)/shard_map/slice | solution.py:121
  12.1 3.6 collective-permute-start
  15.7 1.3 collective-permute-start.1
  17.1 0.1 copy.5
  17.2 0.8 reshape.14.index
  18.0 23.4 %copy.6.generator = bf16[256,64,448]{2,1,0:T(8,128)(2,1)} copy(bf16[256,64,448]{0,2,1:T(8,128)(2,1)} %param.3) | data formatting | bytes 29360128 | tf_op args[0]
  41.4 0.0 collective-permute-done.before
  41.4 0.0 collective-permute-done.1.after
  41.4 26.1 %shard_map.37 = (bf16[16384,128]{1,0:T(8,128)(2,1)}, bf16[16384,128]{1,0:T(8,128)(2,1)}) custom-call(s32[1792]{0:T(1024)} %reshape.14.index, bf16[8192,256]{1,0:T(8,128)(2,1)} %collective-permute-done.before, bf16[16384,256]{1,0:T(8,128)(2,1)} %own.1, bf16[8192,256]{1,0:T(8,128)(2,1)} %collective-permute-done.1.after, bf16[256,64,448]{2,1,0:T(8,128)(2,1)} %copy.6.generator), custom_call_target="tpu_custom_call" | custom-call | flops 3758096384 | bytes 50331648 | tf_op jit(solution)/shard_map/pallas_call | solution.py:50
  67.5 122.9 %all-to-all-done.left = bf16[4,4096,256]{2,1,0:T(8,128)(2,1)} async-done(((bf16[4,4096,256]{2,1,0:T(8,128)(2,1)}), bf16[4,4096,256]{2,1,0:T(8,128)(2,1)}, u32[]{:S(2)}, u32[]{:S(2)}) %all-to-all-start) | async-done | bytes 8388640 | tf_op jit(solution)/shard_map/all_to_all | solution.py:128
  190.4 98.5 %all_to_all.25.right = bf16[4,4096,128]{2,1,0:T(8,128)(2,1)} all-to-all(bf16[4,4096,128]{2,1,0:T(8,128)(2,1)} %bitcast.22), channel_id=1, replica_groups=mesh['rows'=8,'cols'=4] {'cols'}, dimensions={0} | all-to-all | bytes 8388608 | tf_op jit(solution)/shard_map/all_to_all | solution.py:128
  289.0 4.8 %all-to-all-start.2 = ((bf16[4,4096,128]{2,1,0:T(8,128)(2,1)}), bf16[4,4096,128]{2,1,0:T(8,128)(2,1)}, u32[]{:S(2)}, u32[]{:S(2)}) async-start(bf16[4,4096,128]{2,1,0:T(8,128)(2,1)} %bitcast.21), calls=%async_computation.2 | async-start | bytes 8388608 | tf_op jit(solution)/shard_map/all_to_all | solution.py:128
  293.8 9.0 %shard_map.38 = bf16[8,4,128,128]{3,2,1,0:T(8,128)(2,1)} custom-call(bf16[4,4096,256]{2,1,0:T(8,128)(2,1)} %all-to-all-done.left, bf16[4,4096,128]{2,1,0:T(8,128)(2,1)} %all_to_all.25.right), custom_call_target="tpu_custom_call" | custom-call | flops 4294967296 | bytes 20971520 | tf_op jit(solution)/shard_map/pallas_call | solution.py:97
  302.8 1.3 dynamic-slice_bitcast_fusion.6
  304.1 0.7 collective-permute-start.8
  304.8 1.8 collective-permute-start.7
  306.6 0.3 collective-permute-start.6
  306.9 1.5 collective-permute-start.5
  308.4 0.2 collective-permute-start.4
  308.6 0.0 collective-permute-done.8
  308.6 1.5 collective-permute-start.3
  310.1 2.5 collective-permute-done.7
  312.7 0.2 collective-permute-done.6
  312.9 8.2 %collective-permute-done.5 = bf16[4,128,128]{2,1,0:T(8,128)(2,1)S(1)} collective-permute-done((bf16[4,128,128]{2,1,0:T(8,128)(2,1)S(1)}, bf16[4,128,128]{2,1,0:T(8,128)(2,1)S(1)}, u32[]{:S(2)}, u32[]{:S(2)}) %collective-permute-start.5) | collective-permute-done | bytes 131104 | tf_op jit(solution)/shard_map/ppermute | solution.py:153
  321.1 1.0 fusion.5
  322.2 63.9 %all-to-all-done.2.right = bf16[4,4096,128]{2,1,0:T(8,128)(2,1)} async-done(((bf16[4,4096,128]{2,1,0:T(8,128)(2,1)}), bf16[4,4096,128]{2,1,0:T(8,128)(2,1)}, u32[]{:S(2)}, u32[]{:S(2)}) %all-to-all-start.2) | async-done | bytes 4194336 | tf_op jit(solution)/shard_map/all_to_all | solution.py:128
  386.1 8.9 %shard_map.39 = bf16[8,4,128,128]{3,2,1,0:T(8,128)(2,1)} custom-call(bf16[4,4096,256]{2,1,0:T(8,128)(2,1)} %all-to-all-done.left, bf16[4,4096,128]{2,1,0:T(8,128)(2,1)} %all-to-all-done.2.right), custom_call_target="tpu_custom_call" | custom-call | flops 4294967296 | bytes 20971520 | tf_op jit(solution)/shard_map/pallas_call | solution.py:97
  395.0 19.0 %all_to_all.26 = bf16[8,4,128,128]{3,2,1,0:T(8,128)(2,1)S(1)} all-to-all(bf16[8,4,128,128]{3,2,1,0:T(8,128)(2,1)} %shard_map.39), channel_id=1, replica_groups=mesh['rows'=8,'cols'=4] {'rows'}, dimensions={0} | all-to-all | bytes 2097152 | tf_op jit(solution)/shard_map/all_to_all | solution.py:155
  414.1 0.1 convert_reduce_fusion
  414.2 16.5 %all_to_all.27 = f32[4,128,256]{2,1,0:T(8,128)S(1)} all-to-all(f32[4,128,256]{2,1,0:T(8,128)S(1)} %pad_maximum_fusion), channel_id=1, replica_groups=mesh['rows'=8,'cols'=4] {'cols'}, dimensions={0} | all-to-all | bytes 1048576 | tf_op jit(solution)/shard_map/all_to_all | solution.py:159
  430.8 0.7 reduce_sum.19
  (8 shorter events, 0.1 us)
Async XLA Ops:
  0.0 190.4 %all-to-all-start = ((bf16[4,4096,256]{2,1,0:T(8,128)(2,1)}), bf16[4,4096,256]{2,1,0:T(8,128)(2,1)}, u32[]{:S(2)}, u32[]{:S(2)}) async-start(bf16[4,4096,256]{2,1,0:T(8,128)(2,1)} %bitcast.20), calls=%async_computation | async-start | bytes 16777216 | tf_op jit(solution)/shard_map/all_to_all | solution.py:128
  6.3 10.7 %copy-start = (s32[256,7]{0,1:T(8,128)S(1)}, s32[256,7]{0,1:T(8,128)}, u32[]{:S(2)}) copy-start(s32[256,7]{0,1:T(8,128)} %param.4) | copy-start | bytes 21508
  12.1 29.3 %collective-permute-start = (bf16[8192,256]{1,0:T(8,128)(2,1)}, bf16[8192,256]{1,0:T(8,128)(2,1)}, u32[]{:S(2)}, u32[]{:S(2)}) collective-permute-start(bf16[8192,256]{1,0:T(8,128)(2,1)} %get-tuple-element.22), channel_id=1, source_target_pairs={{0,4},{4,8},{8,12},{12,16},{16,20},{20,24},{24,28},{1,5},{5,9},{9,... | collective-permute-start | bytes 12582920 | tf_op jit(solution)/shard_map/ppermute | solution.py:120
  15.7 25.7 %collective-permute-start.1 = (bf16[8192,256]{1,0:T(8,128)(2,1)}, bf16[8192,256]{1,0:T(8,128)(2,1)}, u32[]{:S(2)}, u32[]{:S(2)}) collective-permute-start(bf16[8192,256]{1,0:T(8,128)(2,1)} %get-tuple-element.21), channel_id=1, source_target_pairs={{4,0},{8,4},{12,8},{16,12},{20,16},{24,20},{28,24},{5,1},{9,5},{13... | collective-permute-start | bytes 12582920 | tf_op jit(solution)/shard_map/ppermute | solution.py:121
  289.0 97.1 %all-to-all-start.2 = ((bf16[4,4096,128]{2,1,0:T(8,128)(2,1)}), bf16[4,4096,128]{2,1,0:T(8,128)(2,1)}, u32[]{:S(2)}, u32[]{:S(2)}) async-start(bf16[4,4096,128]{2,1,0:T(8,128)(2,1)} %bitcast.21), calls=%async_computation.2 | async-start | bytes 8388608 | tf_op jit(solution)/shard_map/all_to_all | solution.py:128
  304.1 4.5 %collective-permute-start.8 = (bf16[4,128,128]{2,1,0:T(8,128)(2,1)S(1)}, bf16[4,128,128]{2,1,0:T(8,128)(2,1)S(1)}, u32[]{:S(2)}, u32[]{:S(2)}) collective-permute-start(bf16[4,128,128]{2,1,0:T(8,128)(2,1)S(1)} %get-tuple-element.24), channel_id=1, source_target_pairs={{0,28},{4,0},{8,4},{12,8},{16,12},{20,16},{24,20},{28,24},{1,29},{... | collective-permute-start | bytes 393224 | tf_op jit(solution)/shard_map/ppermute | solution.py:153
  304.8 7.9 %collective-permute-start.7 = (bf16[4,128,128]{2,1,0:T(8,128)(2,1)S(1)}, bf16[4,128,128]{2,1,0:T(8,128)(2,1)S(1)}, u32[]{:S(2)}, u32[]{:S(2)}) collective-permute-start(bf16[4,128,128]{2,1,0:T(8,128)(2,1)S(1)} %get-tuple-element.25), channel_id=1, source_target_pairs={{0,24},{4,28},{8,0},{12,4},{16,8},{20,12},{24,16},{28,20},{1,25},{... | collective-permute-start | bytes 393224 | tf_op jit(solution)/shard_map/ppermute | solution.py:153
  306.6 6.3 %collective-permute-start.6 = (bf16[4,128,128]{2,1,0:T(8,128)(2,1)S(1)}, bf16[4,128,128]{2,1,0:T(8,128)(2,1)S(1)}, u32[]{:S(2)}, u32[]{:S(2)}) collective-permute-start(bf16[4,128,128]{2,1,0:T(8,128)(2,1)S(1)} %get-tuple-element.26), channel_id=1, source_target_pairs={{0,20},{4,24},{8,28},{12,0},{16,4},{20,8},{24,12},{28,16},{1,21},{... | collective-permute-start | bytes 393224 | tf_op jit(solution)/shard_map/ppermute | solution.py:153
  306.9 14.2 %collective-permute-start.5 = (bf16[4,128,128]{2,1,0:T(8,128)(2,1)S(1)}, bf16[4,128,128]{2,1,0:T(8,128)(2,1)S(1)}, u32[]{:S(2)}, u32[]{:S(2)}) collective-permute-start(bf16[4,128,128]{2,1,0:T(8,128)(2,1)S(1)} %get-tuple-element.27), channel_id=1, source_target_pairs={{0,16},{4,20},{8,24},{12,28},{16,0},{20,4},{24,8},{28,12},{1,17},{... | collective-permute-start | bytes 393224 | tf_op jit(solution)/shard_map/ppermute | solution.py:153
  308.4 12.7 %collective-permute-start.4 = (bf16[4,128,128]{2,1,0:T(8,128)(2,1)S(1)}, bf16[4,128,128]{2,1,0:T(8,128)(2,1)S(1)}, u32[]{:S(2)}, u32[]{:S(2)}) collective-permute-start(bf16[4,128,128]{2,1,0:T(8,128)(2,1)S(1)} %get-tuple-element.28), channel_id=1, source_target_pairs={{0,12},{4,16},{8,20},{12,24},{16,28},{20,0},{24,4},{28,8},{1,13},{... | collective-permute-start | bytes 393224 | tf_op jit(solution)/shard_map/ppermute | solution.py:153
  308.6 12.5 %collective-permute-start.3 = (bf16[4,128,128]{2,1,0:T(8,128)(2,1)S(1)}, bf16[4,128,128]{2,1,0:T(8,128)(2,1)S(1)}, u32[]{:S(2)}, u32[]{:S(2)}) collective-permute-start(bf16[4,128,128]{2,1,0:T(8,128)(2,1)S(1)} %get-tuple-element.29), channel_id=1, source_target_pairs={{0,8},{4,12},{8,16},{12,20},{16,24},{20,28},{24,0},{28,4},{1,9},{5... | collective-permute-start | bytes 393224 | tf_op jit(solution)/shard_map/ppermute | solution.py:153
  312.7 8.5 %collective-permute-start.2 = (bf16[4,128,128]{2,1,0:T(8,128)(2,1)S(1)}, bf16[4,128,128]{2,1,0:T(8,128)(2,1)S(1)}, u32[]{:S(2)}, u32[]{:S(2)}) collective-permute-start(bf16[4,128,128]{2,1,0:T(8,128)(2,1)S(1)} %get-tuple-element.23), channel_id=1, source_target_pairs={{0,4},{4,8},{8,12},{12,16},{16,20},{20,24},{24,28},{28,0},{1,5},{5... | collective-permute-start | bytes 393224 | tf_op jit(solution)/shard_map/ppermute | solution.py:153

commit v4 on v3

--- a/solution.py
+++ b/solution.py
@@ -108,6 +108,21 @@
     )(left, right)
 
 
+def summed(partial, axis):
+    shares = lax.all_to_all(partial, axis, split_axis=0, concat_axis=0)
+    return jnp.sum(shares.astype(jnp.float32), axis=0)
+
+
+def summed_by_permutes(partial, axis):
+    me, size = lax.axis_index(axis), lax.axis_size(axis)
+    mine = lax.dynamic_index_in_dim(partial, me, 0, keepdims=False).astype(jnp.float32)
+    for away in range(1, size):
+        piece = lax.dynamic_index_in_dim(partial, lax.rem(me + away, size), 0, keepdims=False)
+        pairs = [(i, (i + away) % size) for i in range(size)]
+        mine += lax.ppermute(piece, axis, pairs).astype(jnp.float32)
+    return mine
+
+
 def body(generator, listed_block_columns, basis):
     brows, bsize, _ = generator.shape
     states, panel = basis.shape
@@ -140,24 +155,14 @@
             slabs[-1] = held
         held = spread(part)
         slabs.append(held)
-    me = lax.axis_index("rows")
     for p, slab in enumerate(slabs):
         if results:
             slab, results[-1] = lax.optimization_barrier((slab, results[-1]))
         partial = product(slab_basis, slab, row_count, col_count)
-        if p + 1 < count:
-            mine = lax.dynamic_index_in_dim(partial, me, 0, keepdims=False).astype(jnp.float32)
-            for away in range(1, row_count):
-                piece = lax.dynamic_index_in_dim(partial, lax.rem(me + away, row_count), 0, keepdims=False)
-                pairs = [(i, (i + away) % row_count) for i in range(row_count)]
-                mine += lax.ppermute(piece, "rows", pairs).astype(jnp.float32)
-        else:
-            shares = lax.all_to_all(partial, "rows", split_axis=0, concat_axis=0)
-            mine = jnp.sum(shares.astype(jnp.float32), axis=0)
-        results.append(mine)
-    share = jnp.concatenate(results, axis=2)
-    pieces = lax.all_to_all(share, "cols", split_axis=0, concat_axis=0)
-    return jnp.sum(pieces, axis=0)
+        for axis in ("rows", "cols"):
+            partial = summed_by_permutes(partial, axis) if p + 1 < count else summed(partial, axis)
+        results.append(partial)
+    return jnp.concatenate(results, axis=1)
 
 
 def solution(mesh):

time: 433 us -> 433 us (level)
  blocking collectives: 134 us -> 128 us
  starting transfers between devices: 22 us -> 26.9 us
    ppermute x7 -> x10, waiting for transfers between devices: 11 us -> 75.5 us  [summed_by_permutes(): mine += lax.ppermute(piece, axis, pairs).astype(jnp.float32)]
    all_to_all x2, waiting for transfers between devices: 187 us -> 123 us  [spread(): return lax.all_to_all(parts, 'cols', split_axis=0, concat_axis=0)]
    all_to_all x2, blocking collectives: 35.6 us -> 29.9 us  [summed(): shares = lax.all_to_all(partial, axis, split_axis=0, concat_axis=0)]
    ppermute x7 -> x10, starting transfers between devices: 5.99 us -> 10.9 us  [summed_by_permutes(): mine += lax.ppermute(piece, axis, pairs).astype(jnp.float32)]
  transfers between devices with their start and end apart: 11 -> 14, of which waited for: 5 -> 6; matrix products, arithmetic and copies ran while one was open for 8% -> 8% of each run, Pallas kernels for 8% -> 8%
where the time goes in v4:
time: 433 us; the launch traced here: 431 us
  waiting for transfers between devices  198 us (46%)
  blocking collectives  128 us (30%)
  Pallas kernels  44 us (10%)
  local copies, waits for them, and re-layouts  31.5 us (7%)
  starting transfers between devices  26.9 us (6%)
    all_to_all x2, waiting for transfers between devices, spread(): return lax.all_to_all(parts, 'cols', split_axis=0, concat_axis=0)  123 us
    all_to_all x1, blocking collectives, spread(): return lax.all_to_all(parts, 'cols', split_axis=0, concat_axis=0)  98.5 us
    ppermute x10, waiting for transfers between devices, summed_by_permutes(): mine += lax.ppermute(piece, axis, pairs).astype(jnp.float32)  75.5 us
    all_to_all x2, blocking collectives, summed(): shares = lax.all_to_all(partial, axis, split_axis=0, concat_axis=0)  29.9 us
    pallas_call x1, Pallas kernels, apply_blocks(): pl.pallas_call(functools.partial(apply_kernel, bsize=bsize, slots=slots,...  26.1 us
    unnamed x3, local copies, waits for them, and re-layouts  23.4 us
    pallas_call x2, Pallas kernels, product(): pl.pallas_call(product_kernel, grid=(depth // tile,), in_specs=specs, out...  17.9 us
    all_to_all x2, starting transfers between devices, spread(): return lax.all_to_all(parts, 'cols', split_axis=0, concat_axis=0)  11.2 us
  transfers between devices with their start and end apart: 14, of which 6 were waited for; matrix products, arithmetic and copies ran while one was open for 8% of the time, Pallas kernels for 8%

profile of v4, /device:TPU:0, one launch (start us, length us, event | category | flops | bytes accessed | tf_op | source)
XLA Modules:
  0.0 431.3 jit_solution(9936487083834197295)
XLA Ops:
  0.0 6.3 %all-to-all-start = ((bf16[4,4096,256]{2,1,0:T(8,128)(2,1)}), bf16[4,4096,256]{2,1,0:T(8,128)(2,1)}, u32[]{:S(2)}, u32[]{:S(2)}) async-start(bf16[4,4096,256]{2,1,0:T(8,128)(2,1)} %bitcast.32), calls=%async_computation | async-start | bytes 16777216 | tf_op jit(solution)/shard_map/all_to_all | solution.py:143
  6.3 5.8 %fusion.8 = (bf16[8192,256]{1,0:T(8,128)(2,1)}, bf16[8192,256]{1,0:T(8,128)(2,1)}) fusion(bf16[16384,256]{1,0:T(8,128)(2,1)} %own.1), kind=kLoop, calls=%fused_computation.23 | loop fusion | bytes 16777216 | tf_op jit(solution)/shard_map/slice | solution.py:136
  12.1 3.6 collective-permute-start
  15.8 1.3 collective-permute-start.1
  17.1 0.1 copy.7
  17.2 0.8 reshape.14.index
  18.0 23.4 %copy.8.generator = bf16[256,64,448]{2,1,0:T(8,128)(2,1)} copy(bf16[256,64,448]{0,2,1:T(8,128)(2,1)} %param.3) | data formatting | bytes 29360128 | tf_op args[0]
  41.4 26.1 %shard_map.37 = (bf16[16384,128]{1,0:T(8,128)(2,1)}, bf16[16384,128]{1,0:T(8,128)(2,1)}) custom-call(s32[1792]{0:T(1024)} %reshape.14.index, bf16[8192,256]{1,0:T(8,128)(2,1)} %collective-permute-done.before, bf16[16384,256]{1,0:T(8,128)(2,1)} %own.1, bf16[8192,256]{1,0:T(8,128)(2,1)} %collective-permute-done.1.after, bf16[256,64,448]{2,1,0:T(8,128)(2,1)} %copy.8.generator), custom_call_target="tpu_custom_call" | custom-call | flops 3758096384 | bytes 50331648 | tf_op jit(solution)/shard_map/pallas_call | solution.py:50
  67.5 122.9 %all-to-all-done.left = bf16[4,4096,256]{2,1,0:T(8,128)(2,1)} async-done(((bf16[4,4096,256]{2,1,0:T(8,128)(2,1)}), bf16[4,4096,256]{2,1,0:T(8,128)(2,1)}, u32[]{:S(2)}, u32[]{:S(2)}) %all-to-all-start) | async-done | bytes 8388640 | tf_op jit(solution)/shard_map/all_to_all | solution.py:143
  190.4 98.5 %all_to_all.25.right = bf16[4,4096,128]{2,1,0:T(8,128)(2,1)} all-to-all(bf16[4,4096,128]{2,1,0:T(8,128)(2,1)} %bitcast.34), channel_id=1, replica_groups=mesh['rows'=8,'cols'=4] {'cols'}, dimensions={0} | all-to-all | bytes 8388608 | tf_op jit(solution)/shard_map/all_to_all | solution.py:143
  289.0 4.8 %all-to-all-start.2 = ((bf16[4,4096,128]{2,1,0:T(8,128)(2,1)}), bf16[4,4096,128]{2,1,0:T(8,128)(2,1)}, u32[]{:S(2)}, u32[]{:S(2)}) async-start(bf16[4,4096,128]{2,1,0:T(8,128)(2,1)} %bitcast.33), calls=%async_computation.2 | async-start | bytes 8388608 | tf_op jit(solution)/shard_map/all_to_all | solution.py:143
  293.9 9.0 %shard_map.38 = bf16[8,4,128,128]{3,2,1,0:T(8,128)(2,1)} custom-call(bf16[4,4096,256]{2,1,0:T(8,128)(2,1)} %all-to-all-done.left, bf16[4,4096,128]{2,1,0:T(8,128)(2,1)} %all_to_all.25.right), custom_call_target="tpu_custom_call" | custom-call | flops 4294967296 | bytes 20971520 | tf_op jit(solution)/shard_map/pallas_call | solution.py:97
  302.8 1.3 dynamic-slice_bitcast_fusion.6
  304.1 0.7 collective-permute-start.8
  304.8 1.8 collective-permute-start.7
  306.6 0.3 collective-permute-start.6
  306.9 1.5 collective-permute-start.5
  308.4 0.2 collective-permute-start.4
  308.6 1.5 collective-permute-start.3
  310.1 2.5 collective-permute-done.7
  312.7 0.2 collective-permute-done.6
  312.9 8.2 %collective-permute-done.5 = bf16[4,128,128]{2,1,0:T(8,128)(2,1)S(1)} collective-permute-done((bf16[4,128,128]{2,1,0:T(8,128)(2,1)S(1)}, bf16[4,128,128]{2,1,0:T(8,128)(2,1)S(1)}, u32[]{:S(2)}, u32[]{:S(2)}) %collective-permute-start.5) | collective-permute-done | bytes 131104 | tf_op jit(solution)/shard_map/ppermute | solution.py:122
  321.1 1.0 fusion.5
  322.2 3.8 collective-permute-start.11
  326.0 1.1 collective-permute-start.9
  327.1 36.2 %collective-permute-done.11 = f32[128,128]{1,0:T(8,128)S(1)} collective-permute-done((f32[128,128]{1,0:T(8,128)S(1)}, f32[128,128]{1,0:T(8,128)S(1)}, u32[]{:S(2)}, u32[]{:S(2)}) %collective-permute-start.11) | collective-permute-done | bytes 65568 | tf_op jit(solution)/shard_map/ppermute | solution.py:122
  363.3 28.3 %collective-permute-done.10 = f32[128,128]{1,0:T(8,128)S(1)} collective-permute-done((f32[128,128]{1,0:T(8,128)S(1)}, f32[128,128]{1,0:T(8,128)S(1)}, u32[]{:S(2)}, u32[]{:S(2)}) %collective-permute-start.10) | collective-permute-done | bytes 65568 | tf_op jit(solution)/shard_map/ppermute | solution.py:122
  391.6 8.9 %shard_map.39 = bf16[8,4,128,128]{3,2,1,0:T(8,128)(2,1)} custom-call(bf16[4,4096,256]{2,1,0:T(8,128)(2,1)} %all-to-all-done.left, bf16[4,4096,128]{2,1,0:T(8,128)(2,1)} %all-to-all-done.2.right), custom_call_target="tpu_custom_call" | custom-call | flops 4294967296 | bytes 20971520 | tf_op jit(solution)/shard_map/pallas_call | solution.py:97
  400.6 19.0 %all_to_all.26 = bf16[8,4,128,128]{3,2,1,0:T(8,128)(2,1)S(1)} all-to-all(bf16[8,4,128,128]{3,2,1,0:T(8,128)(2,1)} %shard_map.39), channel_id=1, replica_groups=mesh['rows'=8,'cols'=4] {'rows'}, dimensions={0} | all-to-all | bytes 2097152 | tf_op jit(solution)/shard_map/all_to_all | solution.py:112
  419.6 0.1 convert_reduce_fusion
  419.8 10.9 %all_to_all.27 = f32[4,128,128]{2,1,0:T(8,128)S(1)} all-to-all(f32[4,128,128]{2,1,0:T(8,128)S(1)} %convert_reduce_fusion), channel_id=1, replica_groups=mesh['rows'=8,'cols'=4] {'cols'}, dimensions={0} | all-to-all | bytes 524288 | tf_op jit(solution)/shard_map/all_to_all | solution.py:112
  430.7 0.7 pad_maximum_fusion
  (16 shorter events, 0.1 us)
Async XLA Ops:
  0.0 190.4 %all-to-all-start = ((bf16[4,4096,256]{2,1,0:T(8,128)(2,1)}), bf16[4,4096,256]{2,1,0:T(8,128)(2,1)}, u32[]{:S(2)}, u32[]{:S(2)}) async-start(bf16[4,4096,256]{2,1,0:T(8,128)(2,1)} %bitcast.32), calls=%async_computation | async-start | bytes 16777216 | tf_op jit(solution)/shard_map/all_to_all | solution.py:143
  6.3 10.7 %copy-start = (s32[256,7]{0,1:T(8,128)S(1)}, s32[256,7]{0,1:T(8,128)}, u32[]{:S(2)}) copy-start(s32[256,7]{0,1:T(8,128)} %param.4) | copy-start | bytes 21508
  12.1 29.3 %collective-permute-start = (bf16[8192,256]{1,0:T(8,128)(2,1)}, bf16[8192,256]{1,0:T(8,128)(2,1)}, u32[]{:S(2)}, u32[]{:S(2)}) collective-permute-start(bf16[8192,256]{1,0:T(8,128)(2,1)} %get-tuple-element.22), channel_id=1, source_target_pairs={{0,4},{4,8},{8,12},{12,16},{16,20},{20,24},{24,28},{1,5},{5,9},{9,... | collective-permute-start | bytes 12582920 | tf_op jit(solution)/shard_map/ppermute | solution.py:135
  15.8 25.7 %collective-permute-start.1 = (bf16[8192,256]{1,0:T(8,128)(2,1)}, bf16[8192,256]{1,0:T(8,128)(2,1)}, u32[]{:S(2)}, u32[]{:S(2)}) collective-permute-start(bf16[8192,256]{1,0:T(8,128)(2,1)} %get-tuple-element.21), channel_id=1, source_target_pairs={{4,0},{8,4},{12,8},{16,12},{20,16},{24,20},{28,24},{5,1},{9,5},{13... | collective-permute-start | bytes 12582920 | tf_op jit(solution)/shard_map/ppermute | solution.py:136
  289.0 102.7 %all-to-all-start.2 = ((bf16[4,4096,128]{2,1,0:T(8,128)(2,1)}), bf16[4,4096,128]{2,1,0:T(8,128)(2,1)}, u32[]{:S(2)}, u32[]{:S(2)}) async-start(bf16[4,4096,128]{2,1,0:T(8,128)(2,1)} %bitcast.33), calls=%async_computation.2 | async-start | bytes 8388608 | tf_op jit(solution)/shard_map/all_to_all | solution.py:143
  304.1 4.5 %collective-permute-start.8 = (bf16[4,128,128]{2,1,0:T(8,128)(2,1)S(1)}, bf16[4,128,128]{2,1,0:T(8,128)(2,1)S(1)}, u32[]{:S(2)}, u32[]{:S(2)}) collective-permute-start(bf16[4,128,128]{2,1,0:T(8,128)(2,1)S(1)} %get-tuple-element.24), channel_id=1, source_target_pairs={{0,28},{4,0},{8,4},{12,8},{16,12},{20,16},{24,20},{28,24},{1,29},{... | collective-permute-start | bytes 393224 | tf_op jit(solution)/shard_map/ppermute | solution.py:122
  304.8 7.9 %collective-permute-start.7 = (bf16[4,128,128]{2,1,0:T(8,128)(2,1)S(1)}, bf16[4,128,128]{2,1,0:T(8,128)(2,1)S(1)}, u32[]{:S(2)}, u32[]{:S(2)}) collective-permute-start(bf16[4,128,128]{2,1,0:T(8,128)(2,1)S(1)} %get-tuple-element.25), channel_id=1, source_target_pairs={{0,24},{4,28},{8,0},{12,4},{16,8},{20,12},{24,16},{28,20},{1,25},{... | collective-permute-start | bytes 393224 | tf_op jit(solution)/shard_map/ppermute | solution.py:122
  306.6 6.3 %collective-permute-start.6 = (bf16[4,128,128]{2,1,0:T(8,128)(2,1)S(1)}, bf16[4,128,128]{2,1,0:T(8,128)(2,1)S(1)}, u32[]{:S(2)}, u32[]{:S(2)}) collective-permute-start(bf16[4,128,128]{2,1,0:T(8,128)(2,1)S(1)} %get-tuple-element.26), channel_id=1, source_target_pairs={{0,20},{4,24},{8,28},{12,0},{16,4},{20,8},{24,12},{28,16},{1,21},{... | collective-permute-start | bytes 393224 | tf_op jit(solution)/shard_map/ppermute | solution.py:122
  306.9 14.2 %collective-permute-start.5 = (bf16[4,128,128]{2,1,0:T(8,128)(2,1)S(1)}, bf16[4,128,128]{2,1,0:T(8,128)(2,1)S(1)}, u32[]{:S(2)}, u32[]{:S(2)}) collective-permute-start(bf16[4,128,128]{2,1,0:T(8,128)(2,1)S(1)} %get-tuple-element.27), channel_id=1, source_target_pairs={{0,16},{4,20},{8,24},{12,28},{16,0},{20,4},{24,8},{28,12},{1,17},{... | collective-permute-start | bytes 393224 | tf_op jit(solution)/shard_map/ppermute | solution.py:122
  308.4 12.7 %collective-permute-start.4 = (bf16[4,128,128]{2,1,0:T(8,128)(2,1)S(1)}, bf16[4,128,128]{2,1,0:T(8,128)(2,1)S(1)}, u32[]{:S(2)}, u32[]{:S(2)}) collective-permute-start(bf16[4,128,128]{2,1,0:T(8,128)(2,1)S(1)} %get-tuple-element.28), channel_id=1, source_target_pairs={{0,12},{4,16},{8,20},{12,24},{16,28},{20,0},{24,4},{28,8},{1,13},{... | collective-permute-start | bytes 393224 | tf_op jit(solution)/shard_map/ppermute | solution.py:122
  308.6 12.5 %collective-permute-start.3 = (bf16[4,128,128]{2,1,0:T(8,128)(2,1)S(1)}, bf16[4,128,128]{2,1,0:T(8,128)(2,1)S(1)}, u32[]{:S(2)}, u32[]{:S(2)}) collective-permute-start(bf16[4,128,128]{2,1,0:T(8,128)(2,1)S(1)} %get-tuple-element.29), channel_id=1, source_target_pairs={{0,8},{4,12},{8,16},{12,20},{16,24},{20,28},{24,0},{28,4},{1,9},{5... | collective-permute-start | bytes 393224 | tf_op jit(solution)/shard_map/ppermute | solution.py:122
  312.7 8.5 %collective-permute-start.2 = (bf16[4,128,128]{2,1,0:T(8,128)(2,1)S(1)}, bf16[4,128,128]{2,1,0:T(8,128)(2,1)S(1)}, u32[]{:S(2)}, u32[]{:S(2)}) collective-permute-start(bf16[4,128,128]{2,1,0:T(8,128)(2,1)S(1)} %get-tuple-element.23), channel_id=1, source_target_pairs={{0,4},{4,8},{8,12},{12,16},{16,20},{20,24},{24,28},{28,0},{1,5},{5... | collective-permute-start | bytes 393224 | tf_op jit(solution)/shard_map/ppermute | solution.py:122
  322.2 41.1 %collective-permute-start.11 = (f32[128,128]{1,0:T(8,128)S(1)}, f32[128,128]{1,0:T(8,128)S(1)}, u32[]{:S(2)}, u32[]{:S(2)}) collective-permute-start(f32[128,128]{1,0:T(8,128)S(1)} %get-tuple-element.31), channel_id=1, source_target_pairs={{0,3},{1,0},{2,1},{3,2},{4,7},{5,4},{6,5},{7,6},{8,11},{9,8},{10,9... | collective-permute-start | bytes 196616 | tf_op jit(solution)/shard_map/ppermute | solution.py:122
  326.0 65.6 %collective-permute-start.10 = (f32[128,128]{1,0:T(8,128)S(1)}, f32[128,128]{1,0:T(8,128)S(1)}, u32[]{:S(2)}, u32[]{:S(2)}) collective-permute-start(f32[128,128]{1,0:T(8,128)S(1)} %get-tuple-element.32), channel_id=1, source_target_pairs={{0,2},{1,3},{2,0},{3,1},{4,6},{5,7},{6,4},{7,5},{8,10},{9,11},{10,... | collective-permute-start | bytes 196616 | tf_op jit(solution)/shard_map/ppermute | solution.py:122
  326.0 65.6 %collective-permute-start.9 = (f32[128,128]{1,0:T(8,128)S(1)}, f32[128,128]{1,0:T(8,128)S(1)}, u32[]{:S(2)}, u32[]{:S(2)}) collective-permute-start(f32[128,128]{1,0:T(8,128)S(1)} %get-tuple-element.30), channel_id=1, source_target_pairs={{0,1},{1,2},{2,3},{3,0},{4,5},{5,6},{6,7},{7,4},{8,9},{9,10},{10,1... | collective-permute-start | bytes 196616 | tf_op jit(solution)/shard_map/ppermute | solution.py:122
